TPU v7x, 32 devices: a whole 2x2x4 slice. The times are simulated.
32 devices in a mesh: groups: 2 (over y), inst: 4 (over x, core), tp: 4 (over z).
Axes of the slice: x: 2, y: 2, z: 4, core: 2. Of those that a mesh axis runs over, the one named last changes fastest.
Arguments:
- prompt_blocks: bfloat16 [256, 2, 128, 1024], P(('groups', 'inst'), None, None, 'tp'), parts along dimension 0, may hold values from -9 to 9
- block_dest: int32 [256], P(('groups', 'inst')), parts along dimension 0, may hold values from 0 to 3, as said below
- block_slot: int32 [256], P(('groups', 'inst')), parts along dimension 0, may hold values from 0 to 63, as said below
- resident_cache: bfloat16 [16, 32, 2, 128, 1024], P(('groups', 'inst'), 'tp'), parts along dimension 0, may hold values from -9 to 9
- queries: bfloat16 [32, 8192], P(('groups', 'inst')), parts along dimension 0, may hold values from -32 to 32
- context_length: int32 [32], P(('groups', 'inst')), parts along dimension 0, may hold values from 1 to 4096, as said below
Outputs:
- attended: bfloat16 [32, 8192], P(('groups', 'inst'), 'tp'), parts along dimension 0
- installed: bfloat16 [16, 32, 2, 128, 1024], P(('groups', 'inst'), 'tp'), parts along dimension 0
There are 2 independent parts, one for each index of `groups`. A program takes and returns all parts, laid end to end along the dimension named above; each array names one. Nothing has to cross between parts.
Inputs may be any that keep to these rules, and one draw needn't show every extreme that they name: `block_dest`: blocks k * 32 to (k + 1) * 32 - 1 are the prompt of instance k. At most 16 blocks of one instance's prompt name the same receiving instance, and in every prompt one receiving instance is named exactly 16 times. `block_slot`: blocks sent to one instance name distinct slots; slot q is page q % 32 of that instance's sequence q // 32. `context_length`: the 2 rows of a sequence are consecutive, their lengths rise by one from step to step, and in every instance one sequence's last row sees all 4096 positions.
All inputs are finite; a program needn't handle non-finite values.
Results may differ from a plain program's by a relative error of at most 0.001.
Values may be sent and summed in bfloat16 or wider, within the bound.
A program may use at most 128 MiB of HBM per device.

v0:
```python
import functools

import jax
import jax.numpy as jnp
from jax import lax
from jax.experimental import pallas as pl
from jax.experimental.pallas import tpu as pltpu
from jax.sharding import PartitionSpec as P

H = 64
KVH = 8
HD = 128
STEPS = 2
GROUP = H // KVH
CORES = 2
PARTS = (1,) * 16
PIECES = len(PARTS)
LEVELS = (10, 11, 12, 16)
SPILL = 2
AHEAD = 5
PAGES_STEP = 4
LANES = 128
MIB = 1024 * 1024

masked_score = -1e30
MESH_ID = pl.DeviceIdType.MESH


def opening_kernel(
    groups, insts, plan_ref, prompt_ref, every_ref, first_ref,
    plan_send, plan_recv, x_send, x_recv, own_send, own_recv, hop_send, hop_recv, local_sem,
):
    group = lax.axis_index("groups")
    me = lax.axis_index("inst")
    core = lax.rem(me, CORES)
    chip = me // CORES
    chips = insts // CORES
    partner = me + 1 - 2 * core
    blocks = prompt_ref.shape[0]
    rows = first_ref.shape[1]
    peers = []
    for g in range(groups):
        for i in range(insts):
            if g or i:
                where = {"groups": lax.rem(group + g, groups), "inst": lax.rem(me + i, insts)}
                peers.append(where)

    barrier = pltpu.get_barrier_semaphore()
    for where in peers:
        pl.semaphore_signal(barrier, inc=1, device_id=where, device_id_type=MESH_ID)
    pl.semaphore_wait(barrier, len(peers))

    def remote(src, dst, send, recv, where):
        return pltpu.make_async_remote_copy(
            src_ref=src, dst_ref=dst, send_sem=send, recv_sem=recv,
            device_id=where, device_id_type=MESH_ID,
        )

    def place(inst):
        return first_ref.at[pl.ds(inst * blocks, blocks)]

    here = group * insts + me
    plans = [
        remote(plan_ref, every_ref.at[here], plan_send.at[i], plan_recv.at[i], where)
        for i, where in enumerate(peers)
    ]
    source = prompt_ref.at[:, pl.ds(0, rows), :]
    crossing = [
        remote(
            source, place(me), x_send.at[s - 1], x_recv.at[s - 1],
            {"inst": lax.rem(chip + s, chips) * CORES + core},
        )
        for s in range(1, chips)
    ]
    own = remote(source, place(me), own_send.at[0], own_recv.at[0], {"inst": partner})
    kept = pltpu.make_async_copy(source, place(me), local_sem.at[0])
    plan_kept = pltpu.make_async_copy(plan_ref, every_ref.at[here], local_sem.at[1])
    for copy in plans + crossing + [own, kept, plan_kept]:
        copy.start()
    hops = []
    for s in range(1, chips):
        crossing[s - 1].wait_recv()
        part = place(lax.rem(chip + chips - s, chips) * CORES + core)
        hops.append(remote(part, part, hop_send.at[s - 1], hop_recv.at[s - 1], {"inst": partner}))
        hops[-1].start()
    kept.wait()
    plan_kept.wait()
    for copy in plans + [own] + hops:
        copy.wait()
    for copy in crossing:
        copy.wait_send()


def opening(plan, prompt, groups, insts, collective_id):
    blocks, rows, width = prompt.shape
    chips = insts // CORES
    peers = groups * insts - 1
    first = rows // sum(PARTS) * PARTS[0]
    dma = pltpu.SemaphoreType.DMA
    return pl.pallas_call(
        functools.partial(opening_kernel, groups, insts),
        out_shape=[
            jax.ShapeDtypeStruct((groups * insts,) + plan.shape, plan.dtype),
            jax.ShapeDtypeStruct((insts * blocks, first, width), prompt.dtype),
        ],
        in_specs=[
            pl.BlockSpec(memory_space=pltpu.VMEM),
            pl.BlockSpec(memory_space=pl.ANY),
        ],
        out_specs=[
            pl.BlockSpec(memory_space=pltpu.VMEM),
            pl.BlockSpec(memory_space=pl.ANY),
        ],
        scratch_shapes=[
            dma((peers,)), dma((peers,)),
            dma((chips - 1,)), dma((chips - 1,)),
            dma((1,)), dma((1,)),
            dma((chips - 1,)), dma((chips - 1,)),
            dma((2,)),
        ],
        compiler_params=pltpu.CompilerParams(
            collective_id=collective_id, has_side_effects=True, vmem_limit_bytes=48 * MIB
        ),
        name="opening",
    )(plan, prompt)


def migrate_kernel(
    insts, tps, share, sent, spill, index_ref, prompt_ref, first_ref, page_ref, packed,
    x_send, x_recv, own_send, own_recv, hop_send, hop_recv,
    z_send, z_recv, back_send, back_recv, home_send, home_recv, pass_send, pass_recv,
    local_sem, keep_sem, *gathered,
):
    me = lax.axis_index("inst")
    tp = lax.axis_index("tp")
    core = lax.rem(me, CORES)
    chip = me // CORES
    chips = insts // CORES
    partner = me + 1 - 2 * core
    blocks, rows, width = prompt_ref.shape
    unit = rows // sum(PARTS)

    def mirror(step):
        return lax.rem(chip + step, chips) * CORES + core

    def tp_peer(step):
        return lax.rem(tp + step, tps)

    barrier = pltpu.get_barrier_semaphore()
    pl.semaphore_signal(barrier, inc=1, device_id={"inst": partner}, device_id_type=MESH_ID)
    for step in range(1, chips):
        pl.semaphore_signal(barrier, inc=1, device_id={"inst": mirror(step)}, device_id_type=MESH_ID)
    for step in range(1, tps):
        pl.semaphore_signal(barrier, inc=1, device_id={"tp": tp_peer(step)}, device_id_type=MESH_ID)
    pl.semaphore_wait(barrier, chips + tps - 1)

    def span(c):
        return pl.ds(sum(PARTS[:c]) * unit, PARTS[c] * unit)

    def remote(src, dst, send, recv, where):
        return pltpu.make_async_remote_copy(
            src_ref=src, dst_ref=dst, send_sem=send, recv_sem=recv,
            device_id=where, device_id_type=MESH_ID,
        )

    def place(inst):
        return pl.ds(inst * blocks, blocks)

    def cross(c):
        src = prompt_ref.at[:, span(c), :]
        dst = gathered[c].at[place(me)]
        return [
            remote(src, dst, x_send.at[c, s - 1], x_recv.at[c, s - 1], {"inst": mirror(s)})
            for s in range(1, chips)
        ]

    def own(c):
        src = prompt_ref.at[:, span(c), :]
        dst = gathered[c].at[place(me)]
        return (
            remote(src, dst, own_send.at[c], own_recv.at[c], {"inst": partner}),
            pltpu.make_async_copy(src, dst, local_sem.at[c]),
        )

    def hop(c, s):
        origin = lax.rem(chip + chips - s, chips) * CORES + core
        part = gathered[c].at[place(origin)]
        return remote(part, part, hop_send.at[c, s - 1], hop_recv.at[c, s - 1], {"inst": partner})

    def spread(c):
        copies = []
        dst = page_ref.at[
            pl.ds(core * share, sent), span(c), pl.ds(pl.multiple_of(tp * width, 128), width)
        ]
        for s in range(1, tps):
            peer = tp_peer(s)
            src = packed.at[pl.ds(peer * sent, sent), span(c), :]
            copies.append(
                remote(src, dst, z_send.at[c, s - 1], z_recv.at[c, s - 1], {"tp": peer})
            )
        kept = packed.at[pl.ds(tp * sent, sent), span(c), :]
        return copies, pltpu.make_async_copy(kept, dst, keep_sem.at[c])

    def back(c):
        part = page_ref.at[pl.ds(core * share, sent), span(c), :]
        return remote(part, part, back_send.at[c], back_recv.at[c], {"inst": partner})

    def home(c):
        src = page_ref.at[pl.ds(core * share + sent - spill, spill), span(c), :]
        dst = page_ref.at[pl.ds(CORES * share + core * spill, spill), span(c), :]
        return remote(src, dst, home_send.at[c], home_recv.at[c], {"inst": mirror(1)})

    def pass_on(c):
        part = page_ref.at[pl.ds(CORES * share + core * spill, spill), span(c), :]
        return remote(part, part, pass_send.at[c], pass_recv.at[c], {"inst": partner})

    def begin(c):
        for copy in cross(c):
            copy.start()
        for copy in own(c):
            copy.start()

    def finish_spread(c):
        copies, kept = spread(c)
        for copy in copies:
            copy.wait_recv()
        kept.wait()
        back(c).start()
        if spill:
            home(c).start()

    def finish_home(c):
        if spill:
            home(c).wait_recv()
            pass_on(c).start()

    first = pltpu.make_async_copy(first_ref, gathered[0], local_sem.at[0])
    first.start()
    for c in range(1, AHEAD):
        begin(c)
    for c in range(PIECES):
        if c and c + AHEAD - 1 < PIECES:
            begin(c + AHEAD - 1)
        if c:
            crossing = cross(c)
            for s in range(1, chips):
                crossing[s - 1].wait_recv()
                hop(c, s).start()
            to_partner, kept = own(c)
            kept.wait()
            to_partner.wait_recv()
            for s in range(1, chips):
                hop(c, s).wait_recv()
        else:
            first.wait()

        def pack(entry, carry):
            chosen = index_ref[entry // sent * share + lax.rem(entry, sent)]
            packed[entry, span(c), :] = gathered[c][chosen]
            return carry

        lax.fori_loop(0, tps * sent, pack, 0, unroll=4)
        copies, kept = spread(c)
        for copy in copies:
            copy.start()
        kept.start()
        if c >= 1:
            finish_spread(c - 1)
        if c >= 2:
            finish_home(c - 2)
    finish_spread(PIECES - 1)
    finish_home(PIECES - 2)
    finish_home(PIECES - 1)
    for c in range(PIECES):
        if c:
            for copy in cross(c):
                copy.wait_send()
            own(c)[0].wait_send()
            for s in range(1, chips):
                hop(c, s).wait_send()
        for copy in spread(c)[0]:
            copy.wait_send()
        back(c).wait()
        if spill:
            home(c).wait_send()
            pass_on(c).wait()


def migrate(insts, tps, share, sent, spill, collective_id, index, prompt, first):
    blocks, rows, width = prompt.shape
    chips = insts // CORES
    dma = pltpu.SemaphoreType.DMA
    return pl.pallas_call(
        functools.partial(migrate_kernel, insts, tps, share, sent, spill),
        out_shape=jax.ShapeDtypeStruct(
            (CORES * (share + SPILL), rows, width * tps), prompt.dtype
        ),
        in_specs=[
            pl.BlockSpec(memory_space=pltpu.SMEM),
            pl.BlockSpec(memory_space=pl.ANY),
            pl.BlockSpec(memory_space=pl.ANY),
        ],
        out_specs=pl.BlockSpec(memory_space=pl.ANY),
        scratch_shapes=[
            pltpu.VMEM((tps * sent, rows, width), prompt.dtype),
            dma((PIECES, chips - 1)), dma((PIECES, chips - 1)),
            dma((PIECES,)), dma((PIECES,)),
            dma((PIECES, chips - 1)), dma((PIECES, chips - 1)),
            dma((PIECES, tps - 1)), dma((PIECES, tps - 1)),
            dma((PIECES,)), dma((PIECES,)),
            dma((PIECES,)), dma((PIECES,)),
            dma((PIECES,)), dma((PIECES,)),
            dma((PIECES,)), dma((PIECES,)),
        ]
        + [
            pltpu.VMEM((insts * blocks, rows // sum(PARTS) * part, width), prompt.dtype)
            for part in PARTS
        ],
        compiler_params=pltpu.CompilerParams(
            collective_id=collective_id, has_side_effects=True, vmem_limit_bytes=48 * MIB
        ),
        name=f"migrate_{sent}",
    )(index, prompt, first)


def attend_kernel(page_local, flag_ref, place_ref, kept_ref, length_ref, base_ref, *refs):
    pages, residents = refs[:PAGES_STEP], refs[PAGES_STEP : 2 * PAGES_STEP]
    query_ref, out_ref, numerator_ref, stat_ref, peak_ref, denominator_ref = refs[2 * PAGES_STEP :]
    step = pl.program_id(0)
    seq = step * PAGES_STEP // page_local
    first = lax.rem(step * PAGES_STEP, page_local)

    for i in range(PAGES_STEP):
        fresh = flag_ref[step * PAGES_STEP + i] > 0

        @pl.when(fresh)
        def _():
            out_ref[i] = pages[i][0]

        @pl.when(jnp.logical_not(fresh))
        def _():
            out_ref[i] = residents[i][0]

    @pl.when(first == 0)
    def _():
        peak_ref[...] = jnp.full(peak_ref.shape, masked_score, jnp.float32)
        denominator_ref[...] = jnp.zeros(denominator_ref.shape, jnp.float32)
        numerator_ref[...] = jnp.zeros(numerator_ref.shape, jnp.float32)

    tokens = out_ref.shape[1] // 2
    scores = jnp.concatenate(
        [
            lax.dot_general(
                query_ref[0],
                out_ref[i, :tokens, :],
                (((1,), (1,)), ((), ())),
                preferred_element_type=jnp.float32,
            )
            for i in range(PAGES_STEP)
        ],
        axis=1,
    ) * HD ** (-0.5)
    row = lax.broadcasted_iota(jnp.int32, scores.shape, 0)
    start = base_ref[0] + first * tokens
    position = start + lax.broadcasted_iota(jnp.int32, scores.shape, 1)
    decode_step = lax.rem(row // GROUP, STEPS)
    limit = jnp.full(scores.shape, length_ref[seq * STEPS], jnp.int32)
    for e in range(1, STEPS):
        limit = jnp.where(decode_step == e, length_ref[seq * STEPS + e], limit)
    usable = position < limit
    old_peak = peak_ref[...]
    best = jnp.max(jnp.where(usable, scores, masked_score), axis=1, keepdims=True)
    peak = jnp.maximum(old_peak, best)
    factor = jnp.exp(old_peak - peak)
    weights = jnp.where(usable, jnp.exp(scores - peak[:, :1]), 0.0)
    denominator = denominator_ref[...] * factor + jnp.sum(weights, axis=1, keepdims=True)
    peak_ref[...] = peak
    denominator_ref[...] = denominator
    high = weights.astype(jnp.bfloat16)
    low = (weights - high.astype(jnp.float32)).astype(jnp.bfloat16)
    rows = STEPS * GROUP
    for v in range(KVH):
        part = slice(v * rows, (v + 1) * rows)
        both = jnp.concatenate([high[part], low[part]], axis=0)
        product = sum(
            jnp.dot(
                both[:, i * tokens : (i + 1) * tokens],
                out_ref[i, tokens:, v * HD : (v + 1) * HD],
                preferred_element_type=jnp.float32,
            )
            for i in range(PAGES_STEP)
        )
        numerator_ref[0, part, :] = (
            numerator_ref[0, part, :] * factor[part] + product[:rows] + product[rows:]
        )

    @pl.when(first == page_local - PAGES_STEP)
    def _():
        lane = lax.broadcasted_iota(jnp.int32, stat_ref.shape, 1)
        spot = lane // (LANES // 4)
        stats = jnp.where(spot == 2 * seq, peak, stat_ref[...])
        stat_ref[...] = jnp.where(spot == 2 * seq + 1, denominator, stats)


def attend(flags, places, kept, lengths, base, pages, resident, queries, seqs):
    total, rows, width = resident.shape
    page_local = total // seqs
    heads = KVH * STEPS * GROUP
    steps_seq = page_local // PAGES_STEP

    def page_spec(which, i):
        return pl.BlockSpec(
            (1, rows, width), lambda s, *scalars: (scalars[which][s * PAGES_STEP + i], 0, 0)
        )

    grid_spec = pltpu.PrefetchScalarGridSpec(
        num_scalar_prefetch=5,
        grid=(total // PAGES_STEP,),
        in_specs=[page_spec(1, i) for i in range(PAGES_STEP)]
        + [page_spec(2, i) for i in range(PAGES_STEP)]
        + [pl.BlockSpec((1, heads, KVH * HD), lambda s, *scalars: (s // steps_seq, 0, 0))],
        out_specs=[
            pl.BlockSpec((PAGES_STEP, rows, width), lambda s, *scalars: (s, 0, 0)),
            pl.BlockSpec((1, heads, HD), lambda s, *scalars: (s // steps_seq, 0, 0)),
            pl.BlockSpec((heads, LANES), lambda s, *scalars: (0, 0)),
        ],
        scratch_shapes=[pltpu.VMEM((heads, LANES), jnp.float32)] * 2,
    )
    return pl.pallas_call(
        functools.partial(attend_kernel, page_local),
        grid_spec=grid_spec,
        out_shape=[
            jax.ShapeDtypeStruct(resident.shape, resident.dtype),
            jax.ShapeDtypeStruct((seqs, heads, HD), jnp.float32),
            jax.ShapeDtypeStruct((heads, LANES), jnp.float32),
        ],
        compiler_params=pltpu.CompilerParams(vmem_limit_bytes=58 * MIB),
        name="attend",
    )(
        flags, places, kept, lengths, base,
        *[pages] * PAGES_STEP, *[resident] * PAGES_STEP, queries,
    )


def combine_kernel(tps, numerator_ref, stat_ref, out_ref, held, held_stat, send_sem, recv_sem, local_sem):
    tp = lax.axis_index("tp")
    seqs, rows = out_ref.shape[:2]
    barrier = pltpu.get_barrier_semaphore()
    for s in range(1, tps):
        pl.semaphore_signal(
            barrier, inc=1, device_id={"tp": lax.rem(tp + s, tps)}, device_id_type=MESH_ID
        )
    pl.semaphore_wait(barrier, tps - 1)
    copies = []
    for s in range(1, tps):
        peer = lax.rem(tp + s, tps)
        part = pl.ds(pl.multiple_of(peer * rows, 8), rows)
        for kind, (src, dst) in enumerate(
            ((numerator_ref.at[:, part, :], held), (stat_ref.at[part, :], held_stat))
        ):
            copies.append(
                pltpu.make_async_remote_copy(
                    src_ref=src,
                    dst_ref=dst.at[s],
                    send_sem=send_sem.at[kind, s - 1],
                    recv_sem=recv_sem.at[kind, s - 1],
                    device_id={"tp": peer},
                    device_id_type=MESH_ID,
                )
            )
    for copy in copies:
        copy.start()
    mine = pl.ds(pl.multiple_of(tp * rows, 8), rows)
    step = LANES // 4
    copies.append(
        pltpu.make_async_copy(numerator_ref.at[:, mine, :], held.at[0], local_sem.at[0])
    )
    copies.append(pltpu.make_async_copy(stat_ref.at[mine, :], held_stat.at[0], local_sem.at[1]))
    for copy in copies[-2:]:
        copy.start()
    for copy in copies:
        copy.wait()
    for seq in range(seqs):
        stats = [held_stat[s] for s in range(tps)]
        tops = [held[s, seq] for s in range(tps)]
        peaks = [part[:, 2 * seq * step : 2 * seq * step + 1] for part in stats]
        lows = [part[:, (2 * seq + 1) * step : (2 * seq + 1) * step + 1] for part in stats]
        peak = functools.reduce(jnp.maximum, peaks)
        factors = [jnp.exp(part - peak) for part in peaks]
        numerator = sum(top * factor for top, factor in zip(tops, factors))
        denominator = sum(low * factor for low, factor in zip(lows, factors))
        out_ref[seq] = (numerator / denominator).astype(out_ref.dtype)


def combine(numerator, stats, tps, collective_id):
    seqs, heads, size = numerator.shape
    rows = heads // tps
    return pl.pallas_call(
        functools.partial(combine_kernel, tps),
        out_shape=jax.ShapeDtypeStruct((seqs, rows, size), jnp.bfloat16),
        in_specs=[pl.BlockSpec(memory_space=pl.ANY)] * 2,
        out_specs=pl.BlockSpec(memory_space=pltpu.VMEM),
        scratch_shapes=[
            pltpu.VMEM((tps, seqs, rows, size), jnp.float32),
            pltpu.VMEM((tps, rows, LANES), jnp.float32),
            pltpu.SemaphoreType.DMA((2, tps - 1)),
            pltpu.SemaphoreType.DMA((2, tps - 1)),
            pltpu.SemaphoreType.DMA((2,)),
        ],
        compiler_params=pltpu.CompilerParams(collective_id=collective_id, has_side_effects=True),
        name="combine",
    )(numerator, stats)


def on_device(prompt_blocks, block_dest, block_slot, resident_cache, queries, context_length):
    insts = lax.axis_size("inst")
    tps = lax.axis_size("tp")
    me = lax.axis_index("inst")
    tp = lax.axis_index("tp")
    blocks, kinds, tokens, width = prompt_blocks.shape
    seqs, page_local = resident_cache.shape[:2]
    pages_seq = page_local * tps
    share = seqs * page_local
    prompt = prompt_blocks.reshape(blocks, kinds * tokens, width)
    plan = jnp.concatenate([block_dest, block_slot])
    plan = jnp.pad(plan[None, :], ((0, 7), (0, -plan.shape[0] % LANES)))
    groups = lax.axis_size("groups")
    plans, first = opening(plan, prompt, groups, insts, len(LEVELS) + 1)
    pairs = plans[:, 0, : 2 * blocks].reshape(groups, insts, 2, blocks).transpose(0, 2, 1, 3)
    pairs = pairs.reshape(groups, 2, insts * blocks)
    load = pairs[:, 0] // CORES * tps + pairs[:, 1] % pages_seq // page_local
    pools = jnp.arange(insts // CORES * tps, dtype=jnp.int32)
    counts = jnp.sum(load[:, :, None] == pools, axis=1, dtype=jnp.int32)
    counts = counts.reshape(groups, insts // CORES, tps)
    spill = SPILL if insts // CORES == 2 else 0
    sizes = sorted({-(-share * level // LEVELS[-1]) for level in LEVELS})
    levels = [(size, spill if size < share else 0) for size in sizes]
    variant = jnp.int32(len(levels) - 1)
    cap = jnp.int32(share)
    for i in reversed(range(len(levels) - 1)):
        size, extra = levels[i]
        over = jnp.maximum(counts - CORES * size, 0)
        room = CORES * size - jnp.minimum(counts, CORES * size)
        fits = jnp.all(over <= jnp.minimum(CORES * extra, room[:, ::-1]))
        variant = jnp.where(fits, i, variant)
        cap = jnp.where(fits, size, cap)
    every = lax.dynamic_index_in_dim(pairs, lax.axis_index("groups"), 0, keepdims=False)
    dest, slot = every[0], every[1]
    total = insts * blocks
    holder = (slot % pages_seq) // page_local
    pool = (dest // CORES) * tps + holder
    order = jnp.arange(total, dtype=jnp.int32)
    rank = jnp.sum(
        jnp.logical_and(pool[:, None] == pool[None, :], order[None, :] < order[:, None]),
        axis=1,
        dtype=jnp.int32,
    )
    entry = jnp.arange(tps * share, dtype=jnp.int32)
    entry_pool = (me // CORES) * tps + entry // share
    entry_rank = (entry % share) * CORES + me % CORES
    hits = jnp.logical_and(pool[None, :] == entry_pool[:, None], rank[None, :] == entry_rank[:, None])
    limit = CORES * cap
    if spill:
        other_pool = (1 - me // CORES) * tps + entry // share
        spilled = rank[None, :] == 2 * limit - 1 - entry_rank[:, None]
        spilled = jnp.logical_and(spilled, (rank >= limit)[None, :])
        spilled = jnp.logical_and(spilled, pool[None, :] == other_pool[:, None])
        hits = jnp.logical_or(hits, spilled)
    index = jnp.sum(jnp.where(hits, order[None, :], 0), axis=1, dtype=jnp.int32)
    local = jnp.arange(share, dtype=jnp.int32)
    wanted = (local // page_local) * pages_seq + tp * page_local + local % page_local
    found = jnp.logical_and(dest[None, :] == me, slot[None, :] == wanted[:, None])
    spot = (rank % CORES) * share + rank // CORES
    if spill:
        slot_at = 2 * limit - 1 - rank
        spot_home = CORES * share + (slot_at % CORES) * spill + slot_at // CORES - cap + spill
        spot = jnp.where(rank >= limit, spot_home, spot)
    places = jnp.sum(jnp.where(found, spot[None, :], 0), axis=1, dtype=jnp.int32)
    flags = jnp.any(found, axis=1).astype(jnp.int32)

    pages = lax.switch(
        variant,
        [
            functools.partial(migrate, insts, tps, share, sent, extra, i)
            for i, (sent, extra) in enumerate(levels)
        ],
        index,
        prompt,
        first,
    )
    place_rows, kept_rows = [], []
    place_now = kept_now = jnp.zeros((PAGES_STEP,), jnp.int32)
    for row in range(share // PAGES_STEP):
        part = slice(row * PAGES_STEP, (row + 1) * PAGES_STEP)
        fresh = flags[part] > 0
        place_now = jnp.where(fresh, places[part], place_now)
        kept_now = jnp.where(fresh, kept_now, local[part])
        place_rows.append(place_now)
        kept_rows.append(kept_now)
    places, kept = jnp.concatenate(place_rows), jnp.concatenate(kept_rows)

    by_head = queries.reshape(seqs, STEPS, KVH, GROUP, HD).transpose(0, 2, 1, 3, 4)
    by_head = by_head.reshape(seqs, KVH, STEPS * GROUP, 1, HD)
    diagonal = jnp.eye(KVH, dtype=jnp.bool_)[None, :, None, :, None]
    wide = jnp.where(diagonal, by_head, jnp.zeros((), queries.dtype))
    wide = wide.reshape(seqs, KVH * STEPS * GROUP, KVH * HD)
    base = (tp * pages_seq // tps * tokens).astype(jnp.int32).reshape(1)
    resident = resident_cache.reshape(share, kinds * tokens, width * tps)
    installed, numerator, stats = attend(
        flags, places, kept, context_length, base, pages, resident, wide, seqs
    )
    merged = combine(numerator, stats, tps, len(LEVELS))
    attended = merged.reshape(seqs, KVH // tps, STEPS, GROUP, HD).transpose(0, 2, 1, 3, 4)
    attended = attended.reshape(seqs * STEPS, H * HD // tps)
    return attended, installed.reshape(resident_cache.shape)


def solution(mesh):
    in_specs = (
        P(("groups", "inst"), None, None, "tp"),
        P(("groups", "inst")),
        P(("groups", "inst")),
        P(("groups", "inst"), "tp", None, None, None),
        P(("groups", "inst"), None),
        P(("groups", "inst")),
    )
    out_specs = (P(("groups", "inst"), "tp"), P(("groups", "inst"), "tp", None, None, None))
    return jax.shard_map(
        on_device, mesh=mesh, in_specs=in_specs, out_specs=out_specs, check_vma=False
    )
```

profile of v0, /device:TPU:0, one launch (start us, length us, event | category | flops | bytes accessed | tf_op | source)
XLA Modules:
  0.0 182.9 jit_solution(3972726849474791382)
XLA Ops:
  0.6 0.7 add_bitcast_fusion
  1.4 12.8 %opening.1 = (s32[8,8,128]{2,1,0:T(8,128)S(1)}, bf16[128,16,256]{2,1,0:T(8,128)(2,1)S(1)}) custom-call(s32[8,128]{1,0:T(8,128)S(1)} %pad.4.plan_ref, bf16[32,256,256]{2,1,0:T(8,128)(2,1)} %bitcast.50), custom_call_target="tpu_custom_call" | custom-call | tf_op jit(solution)/shard_map/opening/pallas_call | solution.py:100
  14.2 0.1 reshape_squeeze.3
  14.3 0.1 reshape.376
  14.5 0.2 fusion.1
  14.6 0.0 copy-start.1
  14.7 0.2 convert_reduce_fusion
  14.9 0.1 convert_reduce_fusion.1
  15.1 0.1 reshape.377
  15.2 0.7 compare_reduce_fusion
  17.9 0.2 select_reduce_fusion.1
  18.0 0.1 compare_select_fusion.16
  18.1 0.7 pad_add_fusion
  20.8 0.2 select_reduce_fusion
  21.0 0.0 copy-start
  21.0 0.0 copy-done.1
  21.0 137.3 %conditional.1 = (bf16[36,256,1024]{2,1,0:T(8,128)(2,1)}) conditional(s32[]{:T(128)} %clamp.3, (s32[64]{0:T(128)S(1)}, bf16[32,256,256]{2,1,0:T(8,128)(2,1)}, bf16[128,16,256]{2,1,0:T(8,128)(2,1)S(1)}) %tuple.42, (s32[64]{0:T(128)S(1)}, bf16[32,256,256]{2,1,0:T(8,128)(2,1)}, ...), branch_computations={%region_8.9_spmd, %region_9.10_spmd, %region_10.11_spmd, %region_1... | conditional | bytes 8 | solution.py:581
  21.0 137.1 %migrate_10.1 = bf16[36,256,1024]{2,1,0:T(8,128)(2,1)} custom-call(s32[64]{0:T(128)S(1)} %get-tuple-element.25.index_ref, bf16[32,256,256]{2,1,0:T(8,128)(2,1)} %get-tuple-element.26.prompt_ref, bf16[128,16,256]{2,1,0:T(8,128)(2,1)S(1)} %get-tuple-element.27.first_ref), custom_call_target="tpu_custom_call" | custom-call | tf_op jit(solution)/shard_map/cond/branch_0_fun/migrate_10/pallas_call | solution.py:293
  158.3 0.0 copy-done
  158.3 0.1 broadcast_in_dim.83
  158.4 0.2 broadcast_in_dim.84
  158.7 0.1 broadcast_in_dim.79
  158.8 0.1 copy.27
  158.9 0.8 broadcast_select_fusion.refs_8_
  159.7 11.1 %attend.1 = (bf16[16,256,1024]{2,1,0:T(8,128)(2,1)}, f32[2,128,128]{2,1,0:T(8,128)}, f32[128,128]{1,0:T(8,128)}) custom-call(s32[16]{0:T(128)} %copy-done.1, s32[16]{0:T(128)} %get-tuple-element.70.place_ref, s32[16]{0:T(128)} %get-tuple-element.71.kept_ref, s32[4]{0:T(128)} %length_ref.1, s32[1]{0:T(128)} %bitcast.7.base_ref, ...), custom_call_target="tpu_custom_call" | custom-call | tf_op jit(solution)/shard_map/attend/pallas_call | solution.py:429
  170.8 10.7 %combine.1 = bf16[2,32,128]{2,1,0:T(8,128)(2,1)} custom-call(f32[2,128,128]{2,1,0:T(8,128)} %get-tuple-element.50.numerator_ref, f32[128,128]{1,0:T(8,128)} %get-tuple-element.51.stat_ref), custom_call_target="tpu_custom_call" | custom-call | tf_op jit(solution)/shard_map/combine/pallas_call | solution.py:498
  181.6 0.7 copy.21
  182.3 0.6 reshape.382
  (23 shorter events, 0.2 us)
Async XLA Ops:
  14.6 6.3 %copy-start.1 = (s32[16]{0:T(128)}, s32[16]{0:T(128)S(1)}, u32[]{:S(2)}) copy-start(s32[16]{0:T(128)S(1)} %convert_element_type.9.flag_ref) | copy-start | bytes 196
  21.0 137.3 %copy-start = (bf16[4,8192]{1,0:T(4,128)(2,1)S(1)}, bf16[4,8192]{1,0:T(4,128)(2,1)}, u32[]{:S(2)}) copy-start(bf16[4,8192]{1,0:T(4,128)(2,1)} %param.14) | copy-start | bytes 196612
where the time goes:
time: 183 us
  Pallas kernels  172 us (94%)
  between operations  4.68 us (3%)
  other arithmetic  4.05 us (2%)
  local copies, waits for them, and re-layouts  2.2 us (1%)
    pallas_call x1, Pallas kernels, migrate(): pl.pallas_call(functools.partial(migrate_kernel, insts, tps, share, sent,...  137 us
    pallas_call x1, Pallas kernels, opening(): pl.pallas_call(functools.partial(opening_kernel, groups, insts), out_shap...  12.8 us
    pallas_call x1, Pallas kernels, attend(): pl.pallas_call(functools.partial(attend_kernel, page_local), grid_spec=gr...  11.1 us
    pallas_call x1, Pallas kernels, combine(): pl.pallas_call(functools.partial(combine_kernel, tps), out_shape=jax.Shap...  10.7 us

commit v1 on v0

--- a/solution.py
+++ b/solution.py
@@ -15,9 +15,10 @@
 CORES = 2
 PARTS = (1,) * 16
 PIECES = len(PARTS)
-LEVELS = (10, 11, 12, 16)
+LEVELS = ((10, 0), (10, 2), (11, 2), (12, 2), (16, 0))
 SPILL = 2
 AHEAD = 5
+HOME_LAG = 6
 PAGES_STEP = 4
 LANES = 128
 MIB = 1024 * 1024
@@ -266,11 +267,11 @@
         kept.start()
         if c >= 1:
             finish_spread(c - 1)
-        if c >= 2:
-            finish_home(c - 2)
+        if c >= HOME_LAG:
+            finish_home(c - HOME_LAG)
     finish_spread(PIECES - 1)
-    finish_home(PIECES - 2)
-    finish_home(PIECES - 1)
+    for c in range(PIECES - HOME_LAG, PIECES):
+        finish_home(c)
     for c in range(PIECES):
         if c:
             for copy in cross(c):
@@ -533,17 +534,18 @@
     counts = jnp.sum(load[:, :, None] == pools, axis=1, dtype=jnp.int32)
     counts = counts.reshape(groups, insts // CORES, tps)
     spill = SPILL if insts // CORES == 2 else 0
-    sizes = sorted({-(-share * level // LEVELS[-1]) for level in LEVELS})
-    levels = [(size, spill if size < share else 0) for size in sizes]
-    variant = jnp.int32(len(levels) - 1)
-    cap = jnp.int32(share)
-    for i in reversed(range(len(levels) - 1)):
-        size, extra = levels[i]
-        over = jnp.maximum(counts - CORES * size, 0)
-        room = CORES * size - jnp.minimum(counts, CORES * size)
-        fits = jnp.all(over <= jnp.minimum(CORES * extra, room[:, ::-1]))
-        variant = jnp.where(fits, i, variant)
-        cap = jnp.where(fits, size, cap)
+    levels = sorted(
+        {(-(-share * size // LEVELS[-1][0]), extra if spill else 0) for size, extra in LEVELS}
+    )
+    sizes = jnp.array([size for size, _ in levels], jnp.int32)
+    extras = jnp.array([extra for _, extra in levels], jnp.int32)
+    full = CORES * sizes[:, None, None, None]
+    over = jnp.maximum(counts[None] - full, 0)
+    room = jnp.maximum(full - counts[None, :, ::-1], 0)
+    short = over > jnp.minimum(CORES * extras[:, None, None, None], room)
+    short = jnp.max(short.astype(jnp.int32), axis=(1, 2, 3))
+    variant = jnp.sum(short)
+    cap = sizes[0] + jnp.sum(short[:-1] * (sizes[1:] - sizes[:-1]))
     every = lax.dynamic_index_in_dim(pairs, lax.axis_index("groups"), 0, keepdims=False)
     dest, slot = every[0], every[1]
     total = insts * blocks

time: 183 us -> 172 us (0.940)
  Pallas kernels: 172 us -> 161 us
  between operations: 4.68 us -> 2.18 us
  other arithmetic: 4.05 us -> 6.03 us
    pallas_call x1, Pallas kernels: 137 us -> 126 us  [migrate(): pl.pallas_call(functools.partial(migrate_kernel, insts, tps, share, sent,...]
    reduce_sum x0 -> x2, other arithmetic: none -> 1.93 us  [the longest x1 1.3 us: on_device(): cap = sizes[0] + jnp.sum(short[:-1] * (sizes[1:] - sizes[:-1]))]
where the time goes in v1:
time: 172 us
  Pallas kernels  161 us (94%)
  other arithmetic  6.03 us (4%)
  local copies, waits for them, and re-layouts  2.2 us (1%)
  between operations  2.18 us (1%)
    pallas_call x1, Pallas kernels, migrate(): pl.pallas_call(functools.partial(migrate_kernel, insts, tps, share, sent,...  126 us
    pallas_call x1, Pallas kernels, opening(): pl.pallas_call(functools.partial(opening_kernel, groups, insts), out_shap...  12.8 us
    pallas_call x1, Pallas kernels, combine(): pl.pallas_call(functools.partial(combine_kernel, tps), out_shape=jax.Shap...  11.1 us
    pallas_call x1, Pallas kernels, attend(): pl.pallas_call(functools.partial(attend_kernel, page_local), grid_spec=gr...  11.1 us

profile of v1, /device:TPU:0, one launch (start us, length us, event | category | flops | bytes accessed | tf_op | source)
XLA Modules:
  0.0 171.6 jit_solution(17264425997929028953)
XLA Ops:
  0.6 0.7 add_bitcast_fusion
  1.4 12.8 %opening.1 = (s32[8,8,128]{2,1,0:T(8,128)S(1)}, bf16[128,16,256]{2,1,0:T(8,128)(2,1)S(1)}) custom-call(s32[8,128]{1,0:T(8,128)S(1)} %pad.4.plan_ref, bf16[32,256,256]{2,1,0:T(8,128)(2,1)} %bitcast.46), custom_call_target="tpu_custom_call" | custom-call | tf_op jit(solution)/shard_map/opening/pallas_call | solution.py:101
  14.2 0.1 reshape_squeeze.3
  14.3 0.1 reshape.380
  14.5 0.2 fusion.2
  14.6 0.0 copy-start.1
  14.7 0.2 convert_reduce_fusion
  14.9 0.1 convert_reduce_fusion.2
  15.1 0.1 sub.122
  15.2 0.8 convert_reduce_fusion.1
  16.0 1.3 multiply_reduce_fusion
  18.0 0.2 select_reduce_fusion.1
  18.1 0.1 compare_select_fusion.16
  18.2 0.7 pad_add_fusion
  18.9 0.6 reduce_sum.58
  20.2 0.2 select_reduce_fusion
  20.4 0.0 copy-start
  20.4 0.0 copy-done.1
  20.4 126.2 %conditional.1 = (bf16[36,256,1024]{2,1,0:T(8,128)(2,1)}) conditional(s32[]{:T(128)} %clamp.3, (s32[64]{0:T(128)S(1)}, bf16[32,256,256]{2,1,0:T(8,128)(2,1)}, bf16[128,16,256]{2,1,0:T(8,128)(2,1)S(1)}) %tuple.44, (s32[64]{0:T(128)S(1)}, bf16[32,256,256]{2,1,0:T(8,128)(2,1)}, ...), branch_computations={%region_8.9_spmd, %region_9.10_spmd, %region_10.11_spmd, %region_1... | conditional | bytes 8 | solution.py:583
  20.5 125.9 %migrate_10.3 = bf16[36,256,1024]{2,1,0:T(8,128)(2,1)} custom-call(s32[64]{0:T(128)S(1)} %get-tuple-element.35.index_ref, bf16[32,256,256]{2,1,0:T(8,128)(2,1)} %get-tuple-element.40.prompt_ref, bf16[128,16,256]{2,1,0:T(8,128)(2,1)S(1)} %get-tuple-element.41.first_ref), custom_call_target="tpu_custom_call" | custom-call | tf_op jit(solution)/shard_map/cond/branch_1_fun/migrate_10/pallas_call | solution.py:294
  146.6 0.0 copy-done
  146.7 0.1 broadcast_in_dim.86
  146.8 0.2 broadcast_in_dim.87
  147.0 0.1 broadcast_in_dim.82
  147.1 0.1 copy.29
  147.2 0.8 broadcast_select_fusion.refs_8_
  148.0 11.1 %attend.1 = (bf16[16,256,1024]{2,1,0:T(8,128)(2,1)}, f32[2,128,128]{2,1,0:T(8,128)}, f32[128,128]{1,0:T(8,128)}) custom-call(s32[16]{0:T(128)} %copy-done.1, s32[16]{0:T(128)} %get-tuple-element.77.place_ref, s32[16]{0:T(128)} %get-tuple-element.78.kept_ref, s32[4]{0:T(128)} %length_ref.1, s32[1]{0:T(128)} %bitcast.7.base_ref, ...), custom_call_target="tpu_custom_call" | custom-call | tf_op jit(solution)/shard_map/attend/pallas_call | solution.py:430
  159.1 11.1 %combine.1 = bf16[2,32,128]{2,1,0:T(8,128)(2,1)} custom-call(f32[2,128,128]{2,1,0:T(8,128)} %get-tuple-element.60.numerator_ref, f32[128,128]{1,0:T(8,128)} %get-tuple-element.61.stat_ref), custom_call_target="tpu_custom_call" | custom-call | tf_op jit(solution)/shard_map/combine/pallas_call | solution.py:499
  170.2 0.7 copy.23
  171.0 0.6 reshape.385
  (23 shorter events, 0.2 us)
Async XLA Ops:
  14.6 5.8 %copy-start.1 = (s32[16]{0:T(128)}, s32[16]{0:T(128)S(1)}, u32[]{:S(2)}) copy-start(s32[16]{0:T(128)S(1)} %convert_element_type.12.flag_ref) | copy-start | bytes 196
  20.4 126.2 %copy-start = (bf16[4,8192]{1,0:T(4,128)(2,1)S(1)}, bf16[4,8192]{1,0:T(4,128)(2,1)}, u32[]{:S(2)}) copy-start(bf16[4,8192]{1,0:T(4,128)(2,1)} %param.17) | copy-start | bytes 196612
